TPU v7x, 256 devices: a whole 4x4x8 slice. The times are simulated.
256 devices in a mesh: seq: 64 (over x, y, z_hi, core), head: 4 (over z_lo).
Axes of the slice: x: 4, y: 4, z: 8 (z_hi: 2, z_lo: 4; z = z_hi * 4 + z_lo), core: 2. Of those that a mesh axis runs over, the one named last changes fastest.
Arguments:
- queries: bfloat16 [12288, 64, 128], P('seq', 'head'), may hold values from -160 to 160
- keys: bfloat16 [12288, 8, 128], P(('seq', 'head')), may hold values from -8 to 8
- values: bfloat16 [12288, 8, 128], P(('seq', 'head')), may hold values from -6 to 6
- doc_ids: int32 [12288], P('seq'), may hold values from 0 to 15, never falling along the last dimension, each value on 1 to 6336 neighbouring positions
Outputs:
- attended: bfloat16 [12288, 64, 128], P('seq', 'head')
Inputs may be any that keep to these rules, and one draw needn't show every extreme that they name: `doc_ids`: documents are runs of consecutive positions; the longest holds exactly 6336 positions.
All inputs are finite; a program needn't handle non-finite values.
Results may differ from a plain program's by a relative error of at most 0.0059.
Values may be sent and summed in bfloat16 or wider, within the bound.
A program may use at most 64 MiB of HBM per device.

v0:
```python
import jax
import jax.numpy as jnp
from jax import lax
from jax.sharding import PartitionSpec as P


def attend(carry, quads, qpos, qids, key_rows, value_rows, id_rows, kstart):
    count = key_rows.shape[0]
    scale = quads.shape[3] ** (-0.5)
    kpos = kstart + jnp.arange(count, dtype=jnp.int32)
    allowed = (
        (kpos[None, :] <= qpos[:, None])
        & (kpos[None, :] >= 0)
        & (id_rows[None, :] == qids[:, None])
    )

    def update(state):
        top, total, summed = state
        scores = (
            jnp.einsum("qkgd,pkd->kgqp", quads, key_rows, preferred_element_type=jnp.float32)
            * scale
        )
        scores = jnp.where(allowed[None, None], scores, -1e30)
        newtop = jnp.maximum(top, jnp.max(scores, axis=-1))
        factor = jnp.exp(top - newtop)
        weights = jnp.where(allowed[None, None], jnp.exp(scores - newtop[..., None]), 0.0)
        total = total * factor + jnp.sum(weights, axis=-1)
        product = jnp.einsum(
            "kgqp,pkd->qkgd",
            weights.astype(jnp.bfloat16),
            value_rows,
            preferred_element_type=jnp.float32,
        )
        summed = summed * jnp.transpose(factor, (2, 0, 1))[..., None] + product
        return (newtop, total, summed)

    return lax.cond(jnp.any(allowed), update, lambda state: state, carry)


def per_device(queries, keys, values, doc_ids):
    rows = queries.shape[0]
    heads_here = queries.shape[1]
    head_dim = queries.shape[2]
    keys_here, values_here = (
        lax.all_to_all(keys, "head", split_axis=1, concat_axis=0, tiled=True),
        lax.all_to_all(values, "head", split_axis=1, concat_axis=0, tiled=True),
    )
    kv_here = keys_here.shape[1]
    group = heads_here // kv_here
    quads = queries.reshape(rows, kv_here, group, head_dim)
    mine = lax.axis_index("seq")
    qpos = mine * rows + jnp.arange(rows, dtype=jnp.int32)
    initial = (
        jnp.full((kv_here, group, rows), -1e30, jnp.float32),
        jnp.zeros((kv_here, group, rows), jnp.float32),
        jnp.zeros((rows, kv_here, group, head_dim), jnp.float32),
    )
    carry = initial
    key_rows = lax.all_gather(keys_here, "seq", axis=0, tiled=True)
    value_rows = lax.all_gather(values_here, "seq", axis=0, tiled=True)
    id_rows = lax.all_gather(doc_ids, "seq", axis=0, tiled=True)
    count = key_rows.shape[0]
    width = min(count, rows)

    def inner(state, index):
        offset = index * width
        key_part = lax.dynamic_slice_in_dim(key_rows, offset, width, 0)
        value_part = lax.dynamic_slice_in_dim(value_rows, offset, width, 0)
        id_part = lax.dynamic_slice_in_dim(id_rows, offset, width, 0)
        return (attend(state, quads, qpos, doc_ids, key_part, value_part, id_part, offset), None)

    carry, unused = lax.scan(inner, carry, jnp.arange(count // width, dtype=jnp.int32))
    top, total, summed = carry
    result = summed / jnp.transpose(total, (2, 0, 1))[..., None]
    return result.reshape(rows, heads_here, head_dim).astype(jnp.bfloat16)


def solution(mesh):
    return jax.shard_map(
        per_device,
        mesh=mesh,
        in_specs=(
            P("seq", "head", None),
            P(("seq", "head"), None, None),
            P(("seq", "head"), None, None),
            P("seq"),
        ),
        out_specs=P("seq", "head", None),
        check_vma=False,
    )
```

profile of v0, /device:TPU:196, one launch (start us, length us, event | category | flops | bytes accessed | tf_op | source)
XLA Modules:
  0.0 776.8 jit_solution(15789499596353756654)
XLA Ops:
  7.5 8.2 %all_to_all.36 = bf16[48,8,128]{2,0,1:T(8,128)(2,1)S(1)} all-to-all(bf16[48,8,128]{2,0,1:T(8,128)(2,1)S(1)} %copy.11), channel_id=1, replica_groups=mesh['seq'=64,'head'=4] {'head'}, dimensions={1} | all-to-all | bytes 196608 | tf_op jit(solution)/shard_map/all_to_all | solution.py:45
  17.3 8.2 %all_to_all.37 = bf16[48,8,128]{2,0,1:T(8,128)(2,1)S(1)} all-to-all(bf16[48,8,128]{2,0,1:T(8,128)(2,1)S(1)} %copy.14), channel_id=1, replica_groups=mesh['seq'=64,'head'=4] {'head'}, dimensions={1} | all-to-all | bytes 196608 | tf_op jit(solution)/shard_map/all_to_all | solution.py:46
  30.3 370.8 %all-reduce = s32[12288]{0:T(1024)S(1)} all-reduce(s32[12288]{0:T(1024)S(1)} %dynamic-update-slice), channel_id=1, replica_groups=mesh['seq'=64,'head'=4] {'seq'}, use_global_device_ids=true, to_apply=%add | all-reduce | flops 12288 | bytes 98304
  401.3 366.7 %while.15 = (s32[]{:T(128)}, f32[2,8,192]{2,1,0:T(8,128)S(1)}, f32[2,8,192]{2,1,0:T(8,128)S(1)}, f32[192,2,8,128]{3,0,2,1:T(8,128)S(1)}, s32[64]{0:T(128)S(1)}, ...) while((s32[]{:T(128)}, f32[2,8,192]{2,1,0:T(8,128)S(1)}, ...), condition=%wide.region_6.7_spmd.clone, body=%wide.region_0.6_spmd.clone.sunk | while | flops 310638336 | bytes 11558621 | solution.py:72
  406.9 5.5 conditional.3
  415.2 5.5 conditional.3
  423.5 5.5 conditional.3
  431.8 5.5 conditional.3
  440.1 5.5 conditional.3
  448.4 5.5 conditional.3
  456.7 5.5 conditional.3
  465.0 5.5 conditional.3
  473.4 5.5 conditional.3
  481.7 5.5 conditional.3
  490.0 5.5 conditional.3
  498.3 5.5 conditional.3
  506.6 5.5 conditional.3
  523.2 5.5 conditional.3
  531.5 5.5 conditional.3
  539.8 5.5 conditional.3
  548.1 5.5 conditional.3
  556.4 5.5 conditional.3
  564.7 5.5 conditional.3
  573.0 5.5 conditional.3
  581.3 5.5 conditional.3
  589.6 5.5 conditional.3
  597.9 5.5 conditional.3
  606.2 5.5 conditional.3
  614.5 5.5 conditional.3
  622.8 5.5 conditional.3
  631.1 5.5 conditional.3
  639.4 5.5 conditional.3
  (582 shorter events, 320.7 us)
Async XLA Ops:
  6.5 394.8 %copy-start = (s32[192]{0:T(256)S(1)}, s32[192]{0:T(256)}, u32[]{:S(2)}) copy-start(s32[192]{0:T(256)} %param.11) | copy-start | bytes 2308
  6.5 394.6 %all-gather.3.cloned.1.call-start = ((), (), s32[]{:S(2)}) async-start(), calls=%async_computation.2 | async-start | bytes 6389760 | tf_op jit(solution)/shard_map/all_gather | solution.py:59
  16.3 384.8 %all-gather.5.cloned.1.call-start = ((), (), s32[]{:S(2)}) async-start(), calls=%async_computation.3 | async-start | bytes 6389760 | tf_op jit(solution)/shard_map/all_gather | solution.py:60
Sparse Core Ops, SparseCore 0:
  16.4 99.1 all-gather.2
  119.3 96.7 all-gather.4
where the time goes:
time: 780 us; the launch traced here: 777 us
  blocking collectives  387 us (50%)
  matrix products  156 us (20%)
  loops' own time  88.2 us (11%)
  other arithmetic  80 us (10%)
  local copies, waits for them, and re-layouts  51 us (7%)
  between operations  14.1 us (2%)
    unnamed x1, blocking collectives  371 us
    dot_general x34, matrix products, update(): jnp.einsum('kgqp,pkd->qkgd', weights.astype(jnp.bfloat16), value_rows, pr...  100 us
    another operation x1, loops' own time, per_device(): lax.scan(inner, carry, jnp.arange(count // width, dtype=jnp.int32))  85.9 us
    dot_general x34, matrix products, update(): jnp.einsum('qkgd,pkd->kgqp', quads, key_rows, preferred_element_type=jnp....  55.9 us
    reduce_or x64, other arithmetic, attend(): return lax.cond(jnp.any(allowed), update, lambda state: state, carry)  50.1 us
    dynamic_slice x64, local copies, waits for them, and re-layouts, per_device(): lax.scan(inner, carry, jnp.arange(count // width, dtype=jnp.int32))  37.5 us
    reduce_sum x34, other arithmetic, update(): total = total * factor + jnp.sum(weights, axis=-1)  28 us
  transfers between devices with their start and end apart: 2, of which 0 were waited for; matrix products, arithmetic and copies ran while one was open for 1% of the time, Pallas kernels for 0%

commit v1 on v0

v1 whole, which is shorter than its diff:
```python
import functools
import math

import jax
import jax.numpy as jnp
from jax import lax
from jax.experimental import pallas as pl
from jax.experimental.pallas import tpu as pltpu
from jax.sharding import PartitionSpec as P

MESH = pl.DeviceIdType.MESH

ROWS = 192
PIECE = 48
GROUP = 8
D = 128
HALF = 2 * ROWS
CHUNK = HALF + 16
KEYS = 2 * HALF
M = 2 * ROWS * GROUP
MC = ROWS * GROUP
SUB = 256
FAR = 2.0**20
SCALE = (1.0 / math.sqrt(D)) * math.log2(math.e)

PLAN = (
    ((1, 0, 1, 1, 1), (1, 1, 0, 0, 1), (1, 3, 0, 1, 0), (2, 0, 0, 0, 0),
     (1, 2, 0, 0, 0), (2, 1, 0, 0, 0), (2, 3, 0, 0, 0), (2, 2, 0, 0, 0)),
    ((0, 0, 0, 1, 0), (1, 1, 1, 1, 1), (1, 0, 0, 0, 0), (1, 2, 0, 0, 0),
     (2, 1, 0, 0, 1), (1, 3, 0, 0, 0), (2, 2, 0, 0, 1), (2, 3, 0, 0, 0)),
    ((0, 1, 0, 1, 0), (1, 2, 1, 1, 1), (0, 0, 0, 0, 0), (1, 1, 0, 0, 0),
     (1, 3, 0, 0, 0), (2, 2, 0, 0, 1), (1, 0, 0, 0, 0), (2, 3, 0, 0, 1)),
    ((0, 2, 0, 0, 0), (0, 0, 0, 0, 0), (1, 3, 1, 1, 1), (0, 1, 0, 0, 0),
     (1, 2, 0, 1, 0), (1, 0, 0, 0, 1), (2, 3, 0, 1, 1), (1, 1, 0, 0, 0)),
)
STEPS = len(PLAN[0])


def packed(field):
    return [sum(step[field] << (2 * k) for k, step in enumerate(lane)) for lane in PLAN]


BACK, LANE, GOX, GOP, GOM = (packed(f) for f in range(5))


def pick(table, y, k):
    value = jnp.int32(table[3])
    for lane in range(3):
        value = jnp.where(y == lane, jnp.int32(table[lane]), value)
    return lax.shift_right_logical(value, 2 * k) & 3


def kernel(q_ref, k_ref, v_ref, id_ref, o_ref,
           wide, snd, kv, qst, qaug, feat, ones, top, acc, obuf,
           zsend, zrecv, lsem, qsend, qrecv, osend, orecv, ssem, rsem, qtr):
    s = lax.axis_index("seq")
    g = lax.axis_index("head")
    x, y, zh, c = s // 16, (s // 4) % 4, (s // 2) % 2, s % 2
    col = s // 4
    low = s % 4

    def at(xx, yy):
        return ((xx * 4 + yy) * 4 + low, g)

    def inside(dz, dc, dg):
        return (col * 4 + ((zh + dz) % 2) * 2 + (c + dc) % 2, (g + dg) % 4)

    sibling = inside(0, 1, 0)
    east = at((x + 1) % 4, y)
    plus = at(x, (y + 1) % 4)
    minus = at(x, (y + 3) % 4)
    others = [(dz, dc, dg) for dz in (0, 1) for dg in (0, 1, 3, 2) for dc in (0, 1) if dz or dc or dg]

    barrier = pltpu.get_barrier_semaphore()
    peers = [inside(*o) for o in others] + [east, at((x + 3) % 4, y), plus, minus]
    for peer in peers:
        pl.semaphore_signal(barrier, inc=1, device_id=peer, device_id_type=MESH)

    for which, ref in enumerate((k_ref, v_ref)):
        wide[...] = ref[...].astype(jnp.float32)
        for h in range(8):
            snd[h, which] = wide[pl.ds(h, PIECE, stride=8), :].astype(jnp.bfloat16)

    ids = id_ref[...].astype(jnp.float32)
    first = ids[:, :D]
    second = jnp.concatenate([ids[:, D:], jnp.zeros((1, 2 * D - ROWS), jnp.float32)], axis=1)
    tile = jnp.concatenate([first, second, jnp.zeros((14, D), jnp.float32)], axis=0)
    block = 2 * zh + c
    kv[col, block, HALF:, :] = tile.astype(jnp.bfloat16)

    pl.semaphore_wait(barrier, len(peers))

    spot = pl.multiple_of(PIECE * g, 16)
    for o in others:
        dz, dc, dg = o
        head = 2 * ((g + dg) % 4) + (c + dc) % 2
        for which in range(2):
            pltpu.make_async_remote_copy(
                src_ref=snd.at[head, which],
                dst_ref=kv.at[col, block, pl.ds(spot + which * ROWS, PIECE)],
                send_sem=zsend.at[dz], recv_sem=zrecv.at[block],
                device_id=inside(*o), device_id_type=MESH).start()
        if dg == 0:
            pltpu.make_async_remote_copy(
                src_ref=kv.at[col, block, pl.ds(HALF, 16)], dst_ref=kv.at[col, block, pl.ds(HALF, 16)],
                send_sem=zsend.at[dz], recv_sem=zrecv.at[block],
                device_id=inside(*o), device_id_type=MESH).start()
    for which in range(2):
        pltpu.make_async_copy(snd.at[2 * g + c, which], kv.at[col, block, pl.ds(spot + which * ROWS, PIECE)],
                              lsem.at[0]).start()

    def wait_rows(sem, n):
        pltpu.make_async_copy(feat.at[pl.ds(0, n)], feat.at[pl.ds(0, n)], sem).wait()

    turned = jnp.transpose(tile[:8])
    lanes = lax.broadcasted_iota(jnp.int32, (D, D), 1).astype(jnp.float32)
    for part, size in ((0, D), (1, ROWS - D)):
        hot = jnp.where(turned[:size, part:part + 1] == lanes[:size], 1.0, 0.0)
        hot = jnp.broadcast_to(hot[:, None, :], (size, GROUP, D)).reshape(size * GROUP, D)
        for which in range(2):
            qst[which, pl.ds(part * D * GROUP, size * GROUP), D:] = hot.astype(jnp.bfloat16)

    def split(t, carry):
        rows = q_ref[pl.ds(t * 16 * 16, 256), :].astype(jnp.float32).reshape(16, 16, D)
        for which in range(2):
            qst[which, pl.ds(t * 128, 128), :D] = (
                rows[:, 8 * which:8 * which + 8, :].reshape(128, D).astype(jnp.bfloat16))
        return carry

    lax.fori_loop(0, ROWS // 16, split, 0)
    base = pl.multiple_of(c * MC, MC)
    qcopy = pltpu.make_async_remote_copy(
        src_ref=qst.at[1 - c], dst_ref=qaug.at[pl.ds(base, MC)],
        send_sem=qsend, recv_sem=qrecv, device_id=sibling, device_id_type=MESH)
    qcopy.start()
    qlocal = pltpu.make_async_copy(qst.at[c], qaug.at[pl.ds(base, MC)], lsem.at[1])
    qlocal.start()
    ones[...] = jnp.ones_like(ones)

    def order(t):
        return 2 * ((zh + t // 2) % 2) + (c + t) % 2

    def hands(step, who, b, gox, gop, gom):
        for direction, (go, target) in enumerate(((gox, east), (gop, plus), (gom, minus))):
            @pl.when(go)
            def _(direction=direction, target=target):
                pltpu.make_async_remote_copy(
                    src_ref=kv.at[who, b], dst_ref=kv.at[who, b],
                    send_sem=ssem.at[step, direction], recv_sem=rsem.at[who, b],
                    device_id=target, device_id_type=MESH).start()

    def handed(step, who, gox, gop, gom):
        for direction, go in enumerate((gox, gop, gom)):
            @pl.when(go)
            def _(direction=direction):
                pltpu.make_async_copy(kv.at[who], kv.at[who], ssem.at[step, direction]).wait()

    own = (x < 3, y < 3, y == 0)

    def quarter(who, target, number):
        return pltpu.make_async_remote_copy(
            src_ref=kv.at[who, 3], dst_ref=kv.at[who, 3],
            send_sem=qtr.at[number], recv_sem=rsem.at[who, 3],
            device_id=target, device_id_type=MESH)

    def block_wait(sem):
        pltpu.make_async_copy(kv.at[0, 0], kv.at[0, 0], sem).wait()

    def features(who, b):
        flip = jnp.transpose(kv[who, b, HALF:, :].astype(jnp.float32)[:8])
        for p, size in ((0, D), (1, ROWS - D)):
            feat[pl.ds(pl.multiple_of(b * ROWS + p * D, 16), size), :] = jnp.where(
                flip[:size, p:p + 1] == lanes[:size], 0.0, -FAR).astype(jnp.bfloat16)

    def scores(r0, keys):
        return lax.dot_general(qaug[pl.ds(r0, SUB), :], keys, (((1,), (1,)), ((), ())),
                               preferred_element_type=jnp.float32)

    def finish(r0, sc, vals, start):
        here = pl.ds(r0, SUB)
        n = sc.shape[1]
        peak = jnp.broadcast_to(jnp.max(sc, axis=1, keepdims=True) * SCALE, (SUB, D))
        if not start:
            old = top[here, :]
            peak = jnp.maximum(old, peak)
        parts = []
        for j in range(0, n, D):
            w = min(D, n - j)
            parts.append(jnp.exp2(sc[:, j:j + w] * SCALE - peak[:, :w]).astype(jnp.bfloat16))
        weights = jnp.concatenate(parts, axis=1)
        out = jnp.dot(weights, vals, preferred_element_type=jnp.float32)
        if start:
            acc[here, :] = out
        else:
            factor = jnp.exp2(old - peak)
            acc[here, :D] = acc[here, :D] * factor + out[:, :D]
            acc[here, D:] = acc[here, D:] * factor + out[:, D:]
        top[here, :] = peak

    def attend(r, who, blocks, start, unroll):
        def keys():
            k = jnp.concatenate([kv[who, b, :ROWS, :] for b in blocks], axis=0)
            f = jnp.concatenate([feat[pl.ds(pl.multiple_of(b * ROWS, 16), ROWS), :] for b in blocks], axis=0)
            return jnp.concatenate([k, f], axis=1)

        def vals():
            v = jnp.concatenate([kv[who, b, ROWS:HALF, :] for b in blocks], axis=0)
            return jnp.concatenate([v, ones[:len(blocks) * ROWS, :]], axis=1)

        sc = scores(r, keys())
        for u in range(unroll):
            here = r + u * SUB
            nxt = scores(here + SUB, keys()) if u + 1 < unroll else None
            if start:
                shape = (SUB, len(blocks) * ROWS)
                row = here + lax.broadcasted_iota(jnp.int32, shape, 0)
                when = lax.broadcasted_iota(jnp.int32, shape, 1)
                sc = jnp.where(when * GROUP <= row, sc, -FAR)
            finish(here, sc, vals(), start)
            sc = nxt

    def sweep(who, blocks, start, count, unroll):
        def body(t, carry):
            attend(pl.multiple_of(t * (SUB * unroll), SUB * unroll), who, blocks, start, unroll)
            return carry

        lax.fori_loop(0, count // (SUB * unroll), body, 0)

    wait_rows(lsem.at[0], 2 * PIECE)
    wait_rows(zrecv.at[block], 6 * PIECE)
    hands(0, col, block, *own)
    block_wait(zrecv.at[order(1)])
    hands(0, col, order(1), *own)
    qlocal.wait()
    qcopy.wait_recv()
    for b in range(2):
        features(col, 2 * zh + b)
    sweep(col, (2 * zh, 2 * zh + 1), True, M, 2)

    for t in (2, 3):
        block_wait(zrecv.at[order(t)])
        hands(0, col, order(t), *own)

    def step_of(k):
        back = pick(BACK, y, k)
        who = (x - back) * 4 + pick(LANE, y, k)
        there = x >= back
        gox = there & (pick(GOX, y, k) > 0) & (x < 3)
        gop = there & (pick(GOP, y, k) > 0)
        gom = there & (pick(GOM, y, k) > 0)
        lone = there & (zh == 0) & (back == 2) & (who % 4 == y) & ((y < 3) | (x == 2))
        return who, there, gox, gop, gom, lone

    def onward(k, t):
        who, there, gox, gop, gom, lone = step_of(k)
        b = order(t)

        @pl.when(gox | gop | gom | lone)
        def _():
            block_wait(rsem.at[who, b])
            hands(k + 1, who, b, gox, gop, gom)

            @pl.when(lone & (b == 3) & (y < 3))
            def _():
                quarter(who, plus, 0).start()

            @pl.when(lone & (b == 3) & (y == 3))
            def _():
                quarter(who, east, 0).start()

    @pl.when(zh == 1)
    def _():
        for b in range(2):
            features(col, b)

    def rest(t, carry):
        onward(0, t)

        @pl.when(zh == 1)
        def _():
            attend(pl.multiple_of(t * (M // 4), SUB), col, (0, 1), False, M // 4 // SUB)

        return carry

    lax.fori_loop(0, 4, rest, 0)

    def step(k, carry):
        who, there, gox, gop, gom, lone = step_of(k)

        @pl.when(there & jnp.logical_not(gox | gop | gom | lone))
        def _():
            for b in range(4):
                block_wait(rsem.at[who, b])

        @pl.when(there)
        def _():
            for b in range(4):
                features(who, b)

        def part(t, carry):
            onward(k + 1, t)

            @pl.when(there)
            def _():
                attend(pl.multiple_of(t * (M // 4), SUB), who, (0, 1, 2, 3), False, M // 4 // SUB)

            return carry

        return lax.fori_loop(0, 4, part, carry)

    lax.fori_loop(0, STEPS, step, 0)

    corner = (zh == 0) & (x == 3)

    @pl.when(corner & (y == 3))
    def _():
        block_wait(rsem.at[3, 3])
        quarter(3, plus, 1).start()

    @pl.when(((zh == 0) & (x >= 2) & (y >= 1)) | (corner & (y == 0)))
    def _():
        who = col - 9
        block_wait(rsem.at[who, 3])
        features(who, 3)
        sweep(who, (3,), False, MC, 2)

    def result(b, slot):
        def body(t, carry):
            here = pl.ds(pl.multiple_of(b * MC + t * 256, 256), 256)
            obuf[slot, pl.ds(t * 256, 256), :] = (acc[here, :D] / acc[here, D:]).astype(jnp.bfloat16)
            return carry

        lax.fori_loop(0, MC // 256, body, 0)

    result(1 - c, c + 2)
    ocopy = pltpu.make_async_remote_copy(
        src_ref=obuf.at[c + 2], dst_ref=obuf.at[c],
        send_sem=osend, recv_sem=orecv, device_id=sibling, device_id_type=MESH)
    ocopy.start()
    result(c, c)
    ocopy.wait_recv()

    def join(t, carry):
        halves = [obuf[which, pl.ds(t * 128, 128), :].astype(jnp.float32).reshape(16, 8, D) for which in range(2)]
        o_ref[pl.ds(t * 256, 256), :] = jnp.concatenate(halves, axis=1).reshape(256, D).astype(jnp.bfloat16)
        return carry

    lax.fori_loop(0, ROWS // 16, join, 0)

    ocopy.wait_send()
    qcopy.wait_send()
    wait_rows(zsend.at[0], 14 * PIECE + 16)
    pltpu.make_async_copy(kv.at[0, pl.ds(0, 2)], kv.at[0, pl.ds(0, 2)], zsend.at[1]).wait()
    handed(0, col, *own)

    def drain(k, carry):
        who, there, gox, gop, gom, lone = step_of(k)
        handed(k + 1, who, gox, gop, gom)

        @pl.when(lone)
        def _():
            block_wait(qtr.at[0])

        return carry

    lax.fori_loop(0, STEPS, drain, 0)

    @pl.when(corner & (y == 3))
    def _():
        block_wait(qtr.at[1])


def per_device(queries, keys, values, doc_ids):
    bf, f32 = jnp.bfloat16, jnp.float32
    dma = pltpu.SemaphoreType.DMA
    vmem = pl.BlockSpec(memory_space=pltpu.VMEM)
    out = pl.pallas_call(
        kernel,
        out_shape=jax.ShapeDtypeStruct((ROWS * 16, D), bf),
        in_specs=[vmem] * 4,
        out_specs=vmem,
        scratch_shapes=[
            pltpu.VMEM((8 * PIECE, D), f32),
            pltpu.VMEM((8, 2, PIECE, D), bf),
            pltpu.VMEM((16, 4, CHUNK, D), bf),
            pltpu.VMEM((2, MC, 2 * D), bf),
            pltpu.VMEM((M, 2 * D), bf),
            pltpu.VMEM((KEYS, D), bf),
            pltpu.VMEM((KEYS, D), bf),
            pltpu.VMEM((M, D), f32),
            pltpu.VMEM((M, 2 * D), f32),
            pltpu.VMEM((4, MC, D), bf),
            dma((2,)), dma((4,)), dma((2,)), dma, dma, dma, dma,
            dma((STEPS + 1, 3)), dma((16, 4)), dma((2,)),
        ],
        compiler_params=pltpu.CompilerParams(
            collective_id=0, has_side_effects=True, vmem_limit_bytes=56 * 1024 * 1024),
    )(queries.reshape(ROWS * 16, D), keys.reshape(8 * PIECE, D), values.reshape(8 * PIECE, D),
      doc_ids.reshape(1, ROWS))
    return out.reshape(ROWS, 16, D)


def solution(mesh):
    return jax.shard_map(
        per_device,
        mesh=mesh,
        in_specs=(
            P("seq", "head", None),
            P(("seq", "head"), None, None),
            P(("seq", "head"), None, None),
            P("seq"),
        ),
        out_specs=P("seq", "head", None),
        check_vma=False,
    )
```

time: 780 us -> 83.2 us (0.11)
  the two profiles are of different devices: /device:TPU:196 before, /device:TPU:39 now
where the time goes in v1:
time: 83.2 us; the launch traced here: 81.6 us
  Pallas kernels  79.4 us (95%)
  local copies, waits for them, and re-layouts  2.15 us (3%)
    pallas_call x1, Pallas kernels, per_device(): pl.pallas_call(kernel, out_shape=jax.ShapeDtypeStruct((ROWS * 16, D), bf)...  79.4 us
    unnamed x1, local copies, waits for them, and re-layouts  2.15 us

profile of v1, /device:TPU:39, one launch (start us, length us, event | category | flops | bytes accessed | tf_op | source)
XLA Modules:
  0.0 81.6 jit_solution(13581361486156517012)
XLA Ops:
  0.0 79.4 %shard_map.46 = bf16[3072,128]{1,0:T(8,128)(2,1)} custom-call(bf16[3072,128]{1,0:T(8,128)(2,1)} %bitcast.6, bf16[384,128]{1,0:T(8,128)(2,1)} %bitcast.7, bf16[384,128]{1,0:T(8,128)(2,1)} %bitcast.8, s32[1,192]{1,0:T(1,128)} %bitcast.9), custom_call_target="tpu_custom_call" | custom-call | tf_op jit(solution)/shard_map/pallas_call | solution.py:377
  79.4 2.1 %copy.6 = bf16[192,16,128]{2,1,0:T(8,128)(2,1)} copy(bf16[192,16,128]{2,1,0:T(8,128)(2,1)} %bitcast.5) | data formatting | bytes 1572864

commit v2 on v1

--- a/solution.py
+++ b/solution.py
@@ -19,7 +19,7 @@
 KEYS = 2 * HALF
 M = 2 * ROWS * GROUP
 MC = ROWS * GROUP
-SUB = 256
+SUB = 768
 FAR = 2.0**20
 SCALE = (1.0 / math.sqrt(D)) * math.log2(math.e)
 
@@ -35,6 +35,13 @@
 )
 STEPS = len(PLAN[0])
 
+ORDER = (
+    (0, 1, 4, 8, 2, 5, 9, 3, 32, 33, 6, 10, 7, 36, 37, 11, 40, 41, 12, 13, 14, 15, 44, 45, 52, 53, 56, 57, 48, 49, 60, 61),
+    (0, 4, 1, 5, 16, 2, 6, 3, 7, 24, 32, 33, 17, 36, 37, 18, 44, 19, 25, 45, 48, 49, 26, 40, 41, 27, 56, 57, 52, 53, 60, 61),
+    (0, 4, 1, 5, 20, 6, 2, 7, 36, 37, 3, 21, 28, 32, 33, 22, 23, 48, 49, 52, 53, 29, 30, 40, 41, 44, 45, 31, 60, 61, 56, 57),
+    (8, 9, 20, 24, 10, 16, 11, 36, 37, 21, 25, 40, 41, 26, 32, 17, 22, 27, 33, 56, 18, 57, 23, 52, 53, 19, 48, 49, 44, 45, 60, 61),
+)
+
 
 def packed(field):
     return [sum(step[field] << (2 * k) for k, step in enumerate(lane)) for lane in PLAN]
@@ -48,6 +55,24 @@
     for lane in range(3):
         value = jnp.where(y == lane, jnp.int32(table[lane]), value)
     return lax.shift_right_logical(value, 2 * k) & 3
+
+
+def plane(bit):
+    words = [sum(((op >> bit) & 1) << i for i, op in enumerate(lane)) for lane in ORDER]
+    return [w - (1 << 32) if w >= 1 << 31 else w for w in words]
+
+
+PLANES = [plane(bit) for bit in range(6)]
+
+
+def fetch(y, i):
+    value = 0
+    for bit, words in enumerate(PLANES):
+        word = jnp.int32(words[3])
+        for lane in range(3):
+            word = jnp.where(y == lane, jnp.int32(words[lane]), word)
+        value = value + (lax.shift_right_logical(word, i) & 1) * (1 << bit)
+    return value
 
 
 def kernel(q_ref, k_ref, v_ref, id_ref, o_ref,
@@ -274,41 +299,46 @@
             features(col, b)
 
     def rest(t, carry):
-        onward(0, t)
-
         @pl.when(zh == 1)
         def _():
-            attend(pl.multiple_of(t * (M // 4), SUB), col, (0, 1), False, M // 4 // SUB)
+            attend(pl.multiple_of(t * (M // 2), SUB), col, (0, 1), False, M // 2 // SUB)
 
         return carry
 
-    lax.fori_loop(0, 4, rest, 0)
-
-    def step(k, carry):
+    lax.fori_loop(0, 2, rest, 0)
+
+    def work(k, t):
         who, there, gox, gop, gom, lone = step_of(k)
 
-        @pl.when(there & jnp.logical_not(gox | gop | gom | lone))
+        @pl.when(there & (t == 0) & jnp.logical_not(gox | gop | gom | lone))
         def _():
             for b in range(4):
                 block_wait(rsem.at[who, b])
 
-        @pl.when(there)
+        @pl.when(there & (t == 0))
         def _():
             for b in range(4):
                 features(who, b)
 
-        def part(t, carry):
-            onward(k + 1, t)
-
-            @pl.when(there)
-            def _():
-                attend(pl.multiple_of(t * (M // 4), SUB), who, (0, 1, 2, 3), False, M // 4 // SUB)
-
-            return carry
-
-        return lax.fori_loop(0, 4, part, carry)
-
-    lax.fori_loop(0, STEPS, step, 0)
+        @pl.when(there)
+        def _():
+            attend(pl.multiple_of(t * (M // 2), SUB), who, (0, 1, 2, 3), False, M // 2 // SUB)
+
+    def turn(i, carry):
+        op = fetch(y, i)
+        k, t = (op // 4) % 8, op % 4
+
+        @pl.when(op < 32)
+        def _():
+            onward(k, t)
+
+        @pl.when(op >= 32)
+        def _():
+            work(k, t)
+
+        return carry
+
+    lax.fori_loop(0, 32, turn, 0)
 
     corner = (zh == 0) & (x == 3)
 

time: 83.2 us -> 76.6 us (0.921); the launches traced: 81.6 us -> 76.5 us
  Pallas kernels: 79.4 us -> 74.4 us
    pallas_call x1, Pallas kernels: 79.4 us -> 74.4 us  [per_device(): pl.pallas_call(kernel, out_shape=jax.ShapeDtypeStruct((ROWS * 16, D), bf)...]
where the time goes in v2:
time: 76.6 us; the launch traced here: 76.5 us
  Pallas kernels  74.4 us (97%)
  local copies, waits for them, and re-layouts  2.15 us (3%)
    pallas_call x1, Pallas kernels, per_device(): pl.pallas_call(kernel, out_shape=jax.ShapeDtypeStruct((ROWS * 16, D), bf)...  74.4 us
    unnamed x1, local copies, waits for them, and re-layouts  2.15 us

profile of v2, /device:TPU:39, one launch (start us, length us, event | category | flops | bytes accessed | tf_op | source)
XLA Modules:
  0.0 76.5 jit_solution(11234778569241245994)
XLA Ops:
  0.0 74.4 %shard_map.46 = bf16[3072,128]{1,0:T(8,128)(2,1)} custom-call(bf16[3072,128]{1,0:T(8,128)(2,1)} %bitcast.6, bf16[384,128]{1,0:T(8,128)(2,1)} %bitcast.7, bf16[384,128]{1,0:T(8,128)(2,1)} %bitcast.8, s32[1,192]{1,0:T(1,128)} %bitcast.9), custom_call_target="tpu_custom_call" | custom-call | tf_op jit(solution)/shard_map/pallas_call | solution.py:407
  74.4 2.1 %copy.6 = bf16[192,16,128]{2,1,0:T(8,128)(2,1)} copy(bf16[192,16,128]{2,1,0:T(8,128)(2,1)} %bitcast.5) | data formatting | bytes 1572864

commit v3 on v2

--- a/solution.py
+++ b/solution.py
@@ -34,12 +34,13 @@
      (1, 2, 0, 1, 0), (1, 0, 0, 0, 1), (2, 3, 0, 1, 1), (1, 1, 0, 0, 0)),
 )
 STEPS = len(PLAN[0])
+RELAY = 22
 
 ORDER = (
-    (0, 1, 4, 8, 2, 5, 9, 3, 32, 33, 6, 10, 7, 36, 37, 11, 40, 41, 12, 13, 14, 15, 44, 45, 52, 53, 56, 57, 48, 49, 60, 61),
-    (0, 4, 1, 5, 16, 2, 6, 3, 7, 24, 32, 33, 17, 36, 37, 18, 44, 19, 25, 45, 48, 49, 26, 40, 41, 27, 56, 57, 52, 53, 60, 61),
-    (0, 4, 1, 5, 20, 6, 2, 7, 36, 37, 3, 21, 28, 32, 33, 22, 23, 48, 49, 52, 53, 29, 30, 40, 41, 44, 45, 31, 60, 61, 56, 57),
-    (8, 9, 20, 24, 10, 16, 11, 36, 37, 21, 25, 40, 41, 26, 32, 17, 22, 27, 33, 56, 18, 57, 23, 52, 53, 19, 48, 49, 44, 45, 60, 61),
+    (0, 1, 34, 35, 64, 4, 8, 5, 9, 258, 2, 12, 13, 326, 3, 282, 6, 10, 14, 15, 455, 7, 11, 309, 398, 445, 415),
+    (0, 4, 1, 5, 34, 258, 35, 64, 16, 17, 326, 2, 6, 24, 3, 7, 25, 385, 18, 316, 19, 377, 26, 421, 27, 475, 495),
+    (0, 4, 1, 5, 34, 258, 35, 64, 20, 21, 394, 6, 7, 28, 323, 2, 22, 364, 3, 23, 29, 283, 489, 30, 31, 343, 509),
+    (8, 9, 34, 258, 35, 64, 20, 24, 16, 21, 25, 330, 10, 454, 11, 17, 309, 26, 27, 385, 18, 22, 478, 19, 23, 411, 383),
 )
 
 
@@ -62,7 +63,7 @@
     return [w - (1 << 32) if w >= 1 << 31 else w for w in words]
 
 
-PLANES = [plane(bit) for bit in range(6)]
+PLANES = [plane(bit) for bit in range(9)]
 
 
 def fetch(y, i):
@@ -116,20 +117,26 @@
     pl.semaphore_wait(barrier, len(peers))
 
     spot = pl.multiple_of(PIECE * g, 16)
-    for o in others:
-        dz, dc, dg = o
-        head = 2 * ((g + dg) % 4) + (c + dc) % 2
-        for which in range(2):
-            pltpu.make_async_remote_copy(
-                src_ref=snd.at[head, which],
-                dst_ref=kv.at[col, block, pl.ds(spot + which * ROWS, PIECE)],
-                send_sem=zsend.at[dz], recv_sem=zrecv.at[block],
-                device_id=inside(*o), device_id_type=MESH).start()
-        if dg == 0:
-            pltpu.make_async_remote_copy(
-                src_ref=kv.at[col, block, pl.ds(HALF, 16)], dst_ref=kv.at[col, block, pl.ds(HALF, 16)],
-                send_sem=zsend.at[dz], recv_sem=zrecv.at[block],
-                device_id=inside(*o), device_id_type=MESH).start()
+
+    def spread(plane):
+        for o in others:
+            dz, dc, dg = o
+            if dz != plane:
+                continue
+            head = 2 * ((g + dg) % 4) + (c + dc) % 2
+            for which in range(2):
+                pltpu.make_async_remote_copy(
+                    src_ref=snd.at[head, which],
+                    dst_ref=kv.at[col, block, pl.ds(spot + which * ROWS, PIECE)],
+                    send_sem=zsend.at[dz], recv_sem=zrecv.at[block],
+                    device_id=inside(*o), device_id_type=MESH).start()
+            if dg == 0:
+                pltpu.make_async_remote_copy(
+                    src_ref=kv.at[col, block, pl.ds(HALF, 16)], dst_ref=kv.at[col, block, pl.ds(HALF, 16)],
+                    send_sem=zsend.at[dz], recv_sem=zrecv.at[block],
+                    device_id=inside(*o), device_id_type=MESH).start()
+
+    spread(0)
     for which in range(2):
         pltpu.make_async_copy(snd.at[2 * g + c, which], kv.at[col, block, pl.ds(spot + which * ROWS, PIECE)],
                               lsem.at[0]).start()
@@ -160,6 +167,7 @@
     qcopy.start()
     qlocal = pltpu.make_async_copy(qst.at[c], qaug.at[pl.ds(base, MC)], lsem.at[1])
     qlocal.start()
+    spread(1)
     ones[...] = jnp.ones_like(ones)
 
     def order(t):
@@ -191,11 +199,11 @@
     def block_wait(sem):
         pltpu.make_async_copy(kv.at[0, 0], kv.at[0, 0], sem).wait()
 
-    def features(who, b):
+    def features(i, who, b, near):
         flip = jnp.transpose(kv[who, b, HALF:, :].astype(jnp.float32)[:8])
         for p, size in ((0, D), (1, ROWS - D)):
-            feat[pl.ds(pl.multiple_of(b * ROWS + p * D, 16), size), :] = jnp.where(
-                flip[:size, p:p + 1] == lanes[:size], 0.0, -FAR).astype(jnp.bfloat16)
+            feat[pl.ds(i * ROWS + p * D, size), :] = jnp.where(
+                flip[:size, p:p + 1] == lanes[:size], near, -FAR).astype(jnp.bfloat16)
 
     def scores(r0, keys):
         return lax.dot_general(qaug[pl.ds(r0, SUB), :], keys, (((1,), (1,)), ((), ())),
@@ -222,31 +230,35 @@
             acc[here, D:] = acc[here, D:] * factor + out[:, D:]
         top[here, :] = peak
 
-    def attend(r, who, blocks, start, unroll):
+    def attend(r, blocks, start, unroll):
+        n = len(blocks) * ROWS
+
         def keys():
-            k = jnp.concatenate([kv[who, b, :ROWS, :] for b in blocks], axis=0)
-            f = jnp.concatenate([feat[pl.ds(pl.multiple_of(b * ROWS, 16), ROWS), :] for b in blocks], axis=0)
-            return jnp.concatenate([k, f], axis=1)
+            k = jnp.concatenate([kv[who, b, :ROWS, :] for who, b in blocks], axis=0)
+            return jnp.concatenate([k, feat[:n, :]], axis=1)
 
         def vals():
-            v = jnp.concatenate([kv[who, b, ROWS:HALF, :] for b in blocks], axis=0)
-            return jnp.concatenate([v, ones[:len(blocks) * ROWS, :]], axis=1)
+            v = jnp.concatenate([kv[who, b, ROWS:HALF, :] for who, b in blocks], axis=0)
+            return jnp.concatenate([v, ones[:n, :]], axis=1)
 
         sc = scores(r, keys())
         for u in range(unroll):
             here = r + u * SUB
             nxt = scores(here + SUB, keys()) if u + 1 < unroll else None
             if start:
-                shape = (SUB, len(blocks) * ROWS)
+                shape = (SUB, n)
                 row = here + lax.broadcasted_iota(jnp.int32, shape, 0)
                 when = lax.broadcasted_iota(jnp.int32, shape, 1)
                 sc = jnp.where(when * GROUP <= row, sc, -FAR)
             finish(here, sc, vals(), start)
             sc = nxt
 
-    def sweep(who, blocks, start, count, unroll):
+    def sweep(blocks, nears, start, count, unroll):
+        for i, ((who, b), near) in enumerate(zip(blocks, nears)):
+            features(i, who, b, near)
+
         def body(t, carry):
-            attend(pl.multiple_of(t * (SUB * unroll), SUB * unroll), who, blocks, start, unroll)
+            attend(pl.multiple_of(t * (SUB * unroll), SUB * unroll), blocks, start, unroll)
             return carry
 
         lax.fori_loop(0, count // (SUB * unroll), body, 0)
@@ -258,13 +270,7 @@
     hands(0, col, order(1), *own)
     qlocal.wait()
     qcopy.wait_recv()
-    for b in range(2):
-        features(col, 2 * zh + b)
-    sweep(col, (2 * zh, 2 * zh + 1), True, M, 2)
-
-    for t in (2, 3):
-        block_wait(zrecv.at[order(t)])
-        hands(0, col, order(t), *own)
+    sweep([(col, 2 * zh), (col, 2 * zh + 1)], [0.0] * 2, True, M, 4)
 
     def step_of(k):
         back = pick(BACK, y, k)
@@ -293,89 +299,73 @@
             def _():
                 quarter(who, east, 0).start()
 
-    @pl.when(zh == 1)
-    def _():
-        for b in range(2):
-            features(col, b)
-
-    def rest(t, carry):
-        @pl.when(zh == 1)
-        def _():
-            attend(pl.multiple_of(t * (M // 2), SUB), col, (0, 1), False, M // 2 // SUB)
-
-        return carry
-
-    lax.fori_loop(0, 2, rest, 0)
-
-    def work(k, t):
-        who, there, gox, gop, gom, lone = step_of(k)
-
-        @pl.when(there & (t == 0) & jnp.logical_not(gox | gop | gom | lone))
-        def _():
-            for b in range(4):
-                block_wait(rsem.at[who, b])
-
-        @pl.when(there & (t == 0))
-        def _():
-            for b in range(4):
-                features(who, b)
-
-        @pl.when(there)
-        def _():
-            attend(pl.multiple_of(t * (M // 2), SUB), who, (0, 1, 2, 3), False, M // 2 // SUB)
+    corner = (zh == 0) & (x == 3)
 
     def turn(i, carry):
         op = fetch(y, i)
-        k, t = (op // 4) % 8, op % 4
 
         @pl.when(op < 32)
         def _():
-            onward(k, t)
-
-        @pl.when(op >= 32)
-        def _():
-            work(k, t)
+            onward(op // 4, op % 4)
+
+        @pl.when((op >= 32) & (op < 64))
+        def _():
+            b = order(op % 4)
+            block_wait(zrecv.at[b])
+            hands(0, col, b, *own)
+
+        @pl.when((op == 64) & (zh == 1))
+        def _():
+            sweep([(col, 0), (col, 1)], [0.0] * 2, False, M, 4)
+
+        blocks, nears, present = [], [], []
+        for pair in ((op % 256) // 16, op % 16):
+            who, there, gox, gop, gom, lone = step_of(pair // 2)
+            pairs = [order(2 * (pair % 2) + j) for j in range(2)]
+
+            @pl.when((op >= 256) & there & jnp.logical_not(gox | gop | gom | lone))
+            def _(who=who, pairs=pairs):
+                for b in pairs:
+                    block_wait(rsem.at[who, b])
+
+            blocks += [(jnp.where(there, who, col), b) for b in pairs]
+            nears += [jnp.where(there, 0.0, -FAR)] * 2
+            present.append(there)
+
+        @pl.when((op >= 256) & (present[0] | present[1]))
+        def _():
+            sweep(blocks, nears, False, M, 4)
+
+        @pl.when((i == RELAY) & corner & (y == 3))
+        def _():
+            block_wait(rsem.at[3, 3])
+            quarter(3, plus, 1).start()
 
         return carry
 
-    lax.fori_loop(0, 32, turn, 0)
-
-    corner = (zh == 0) & (x == 3)
-
-    @pl.when(corner & (y == 3))
-    def _():
-        block_wait(rsem.at[3, 3])
-        quarter(3, plus, 1).start()
+    lax.fori_loop(0, len(ORDER[0]), turn, 0)
 
     @pl.when(((zh == 0) & (x >= 2) & (y >= 1)) | (corner & (y == 0)))
     def _():
         who = col - 9
         block_wait(rsem.at[who, 3])
-        features(who, 3)
-        sweep(who, (3,), False, MC, 2)
-
-    def result(b, slot):
+        sweep([(who, 3)], [0.0], False, MC, 2)
+
+    def result(b, ref, slot):
         def body(t, carry):
             here = pl.ds(pl.multiple_of(b * MC + t * 256, 256), 256)
-            obuf[slot, pl.ds(t * 256, 256), :] = (acc[here, :D] / acc[here, D:]).astype(jnp.bfloat16)
+            ref[slot, pl.ds(t * 256, 256), :] = (acc[here, :D] / acc[here, D:]).astype(jnp.bfloat16)
             return carry
 
         lax.fori_loop(0, MC // 256, body, 0)
 
-    result(1 - c, c + 2)
+    result(1 - c, obuf, 0)
     ocopy = pltpu.make_async_remote_copy(
-        src_ref=obuf.at[c + 2], dst_ref=obuf.at[c],
+        src_ref=obuf.at[0], dst_ref=o_ref.at[c],
         send_sem=osend, recv_sem=orecv, device_id=sibling, device_id_type=MESH)
     ocopy.start()
-    result(c, c)
+    result(c, o_ref, c)
     ocopy.wait_recv()
-
-    def join(t, carry):
-        halves = [obuf[which, pl.ds(t * 128, 128), :].astype(jnp.float32).reshape(16, 8, D) for which in range(2)]
-        o_ref[pl.ds(t * 256, 256), :] = jnp.concatenate(halves, axis=1).reshape(256, D).astype(jnp.bfloat16)
-        return carry
-
-    lax.fori_loop(0, ROWS // 16, join, 0)
 
     ocopy.wait_send()
     qcopy.wait_send()
@@ -406,7 +396,7 @@
     vmem = pl.BlockSpec(memory_space=pltpu.VMEM)
     out = pl.pallas_call(
         kernel,
-        out_shape=jax.ShapeDtypeStruct((ROWS * 16, D), bf),
+        out_shape=jax.ShapeDtypeStruct((2, MC, D), bf),
         in_specs=[vmem] * 4,
         out_specs=vmem,
         scratch_shapes=[
@@ -419,7 +409,7 @@
             pltpu.VMEM((KEYS, D), bf),
             pltpu.VMEM((M, D), f32),
             pltpu.VMEM((M, 2 * D), f32),
-            pltpu.VMEM((4, MC, D), bf),
+            pltpu.VMEM((1, MC, D), bf),
             dma((2,)), dma((4,)), dma((2,)), dma, dma, dma, dma,
             dma((STEPS + 1, 3)), dma((16, 4)), dma((2,)),
         ],
@@ -427,7 +417,7 @@
             collective_id=0, has_side_effects=True, vmem_limit_bytes=56 * 1024 * 1024),
     )(queries.reshape(ROWS * 16, D), keys.reshape(8 * PIECE, D), values.reshape(8 * PIECE, D),
       doc_ids.reshape(1, ROWS))
-    return out.reshape(ROWS, 16, D)
+    return jnp.swapaxes(out.reshape(2, ROWS, GROUP, D), 0, 1).reshape(ROWS, 2 * GROUP, D)
 
 
 def solution(mesh):

time: 76.6 us -> 67.8 us (0.89)
  Pallas kernels: 74.4 us -> 65.5 us
    pallas_call x1, Pallas kernels: 74.4 us -> 65.5 us  [per_device(): pl.pallas_call(kernel, out_shape=jax.ShapeDtypeStruct((2, MC, D), bf), in...]
    reshape x0 -> x1, local copies, waits for them, and re-layouts: none -> 2.15 us  [per_device(): jnp.swapaxes(out.reshape(2, ROWS, GROUP, D), 0, 1)]
    unnamed x1 -> x0, local copies, waits for them, and re-layouts: 2.15 us -> none
where the time goes in v3:
time: 67.8 us; the launch traced here: 67.7 us
  Pallas kernels  65.5 us (97%)
  local copies, waits for them, and re-layouts  2.15 us (3%)
    pallas_call x1, Pallas kernels, per_device(): pl.pallas_call(kernel, out_shape=jax.ShapeDtypeStruct((2, MC, D), bf), in...  65.5 us
    reshape x1, local copies, waits for them, and re-layouts, per_device(): jnp.swapaxes(out.reshape(2, ROWS, GROUP, D), 0, 1)  2.15 us

profile of v3, /device:TPU:39, one launch (start us, length us, event | category | flops | bytes accessed | tf_op | source)
XLA Modules:
  0.0 67.7 jit_solution(7382982050088400627)
XLA Ops:
  0.0 65.5 %shard_map.46 = bf16[2,1536,128]{2,1,0:T(8,128)(2,1)} custom-call(bf16[3072,128]{1,0:T(8,128)(2,1)} %bitcast.11, bf16[384,128]{1,0:T(8,128)(2,1)} %bitcast.12, bf16[384,128]{1,0:T(8,128)(2,1)} %bitcast.13, s32[1,192]{1,0:T(1,128)} %bitcast.14), custom_call_target="tpu_custom_call" | custom-call | tf_op jit(solution)/shard_map/pallas_call | solution.py:397
  65.5 2.1 %copy_bitcast_fusion = bf16[192,16,128]{2,1,0:T(8,128)(2,1)} fusion(bf16[2,1536,128]{2,1,0:T(8,128)(2,1)} %shard_map.46), kind=kLoop, calls=%fused_computation | loop fusion | bytes 1572864 | tf_op jit(solution)/shard_map/reshape | solution.py:420

commit v4 on v3

--- a/solution.py
+++ b/solution.py
@@ -35,6 +35,7 @@
 )
 STEPS = len(PLAN[0])
 RELAY = 22
+LATE = 21
 
 ORDER = (
     (0, 1, 34, 35, 64, 4, 8, 5, 9, 258, 2, 12, 13, 326, 3, 282, 6, 10, 14, 15, 455, 7, 11, 309, 398, 445, 415),
@@ -51,11 +52,18 @@
 BACK, LANE, GOX, GOP, GOM = (packed(f) for f in range(5))
 
 
-def pick(table, y, k):
-    value = jnp.int32(table[3])
-    for lane in range(3):
-        value = jnp.where(y == lane, jnp.int32(table[lane]), value)
-    return lax.shift_right_logical(value, 2 * k) & 3
+def by_lane(tables, y):
+    words = []
+    for table in tables:
+        word = jnp.int32(table[3])
+        for lane in range(3):
+            word = jnp.where(y == lane, jnp.int32(table[lane]), word)
+        words.append(word)
+    return words
+
+
+def pick(word, k):
+    return lax.shift_right_logical(word, 2 * k) & 3
 
 
 def plane(bit):
@@ -66,12 +74,9 @@
 PLANES = [plane(bit) for bit in range(9)]
 
 
-def fetch(y, i):
+def fetch(words, i):
     value = 0
-    for bit, words in enumerate(PLANES):
-        word = jnp.int32(words[3])
-        for lane in range(3):
-            word = jnp.where(y == lane, jnp.int32(words[lane]), word)
+    for bit, word in enumerate(words):
         value = value + (lax.shift_right_logical(word, i) & 1) * (1 << bit)
     return value
 
@@ -95,7 +100,7 @@
     east = at((x + 1) % 4, y)
     plus = at(x, (y + 1) % 4)
     minus = at(x, (y + 3) % 4)
-    others = [(dz, dc, dg) for dz in (0, 1) for dg in (0, 1, 3, 2) for dc in (0, 1) if dz or dc or dg]
+    others = [(dz, dc, dg) for dz in (0, 1) for dc in (0, 1) for dg in (2, 1, 3, 0) if dz or dc or dg]
 
     barrier = pltpu.get_barrier_semaphore()
     peers = [inside(*o) for o in others] + [east, at((x + 3) % 4, y), plus, minus]
@@ -105,7 +110,7 @@
     for which, ref in enumerate((k_ref, v_ref)):
         wide[...] = ref[...].astype(jnp.float32)
         for h in range(8):
-            snd[h, which] = wide[pl.ds(h, PIECE, stride=8), :].astype(jnp.bfloat16)
+            snd[h, which * PIECE:(which + 1) * PIECE, :] = wide[pl.ds(h, PIECE, stride=8), :].astype(jnp.bfloat16)
 
     ids = id_ref[...].astype(jnp.float32)
     first = ids[:, :D]
@@ -116,30 +121,21 @@
 
     pl.semaphore_wait(barrier, len(peers))
 
-    spot = pl.multiple_of(PIECE * g, 16)
-
-    def spread(plane):
-        for o in others:
-            dz, dc, dg = o
-            if dz != plane:
-                continue
-            head = 2 * ((g + dg) % 4) + (c + dc) % 2
-            for which in range(2):
-                pltpu.make_async_remote_copy(
-                    src_ref=snd.at[head, which],
-                    dst_ref=kv.at[col, block, pl.ds(spot + which * ROWS, PIECE)],
-                    send_sem=zsend.at[dz], recv_sem=zrecv.at[block],
-                    device_id=inside(*o), device_id_type=MESH).start()
-            if dg == 0:
-                pltpu.make_async_remote_copy(
-                    src_ref=kv.at[col, block, pl.ds(HALF, 16)], dst_ref=kv.at[col, block, pl.ds(HALF, 16)],
-                    send_sem=zsend.at[dz], recv_sem=zrecv.at[block],
-                    device_id=inside(*o), device_id_type=MESH).start()
-
-    spread(0)
-    for which in range(2):
-        pltpu.make_async_copy(snd.at[2 * g + c, which], kv.at[col, block, pl.ds(spot + which * ROWS, PIECE)],
-                              lsem.at[0]).start()
+    spot = pl.ds(pl.multiple_of(2 * PIECE * g, 16), 2 * PIECE)
+
+    for o in others:
+        dz, dc, dg = o
+        head = 2 * ((g + dg) % 4) + (c + dc) % 2
+        pltpu.make_async_remote_copy(
+            src_ref=snd.at[head], dst_ref=kv.at[col, block, spot],
+            send_sem=zsend.at[dz], recv_sem=zrecv.at[block],
+            device_id=inside(*o), device_id_type=MESH).start()
+        if dg == 0:
+            pltpu.make_async_remote_copy(
+                src_ref=kv.at[col, block, pl.ds(HALF, 16)], dst_ref=kv.at[col, block, pl.ds(HALF, 16)],
+                send_sem=zsend.at[dz], recv_sem=zrecv.at[block],
+                device_id=inside(*o), device_id_type=MESH).start()
+    pltpu.make_async_copy(snd.at[2 * g + c], kv.at[col, block, spot], lsem.at[0]).start()
 
     def wait_rows(sem, n):
         pltpu.make_async_copy(feat.at[pl.ds(0, n)], feat.at[pl.ds(0, n)], sem).wait()
@@ -167,7 +163,6 @@
     qcopy.start()
     qlocal = pltpu.make_async_copy(qst.at[c], qaug.at[pl.ds(base, MC)], lsem.at[1])
     qlocal.start()
-    spread(1)
     ones[...] = jnp.ones_like(ones)
 
     def order(t):
@@ -234,11 +229,13 @@
         n = len(blocks) * ROWS
 
         def keys():
-            k = jnp.concatenate([kv[who, b, :ROWS, :] for who, b in blocks], axis=0)
+            k = jnp.concatenate([kv[who, b, r0:r0 + PIECE, :] for who, b in blocks
+                                 for r0 in range(0, HALF, 2 * PIECE)], axis=0)
             return jnp.concatenate([k, feat[:n, :]], axis=1)
 
         def vals():
-            v = jnp.concatenate([kv[who, b, ROWS:HALF, :] for who, b in blocks], axis=0)
+            v = jnp.concatenate([kv[who, b, r0:r0 + PIECE, :] for who, b in blocks
+                                 for r0 in range(PIECE, HALF, 2 * PIECE)], axis=0)
             return jnp.concatenate([v, ones[:n, :]], axis=1)
 
         sc = scores(r, keys())
@@ -253,9 +250,12 @@
             finish(here, sc, vals(), start)
             sc = nxt
 
-    def sweep(blocks, nears, start, count, unroll):
+    def mark(blocks, nears):
         for i, ((who, b), near) in enumerate(zip(blocks, nears)):
             features(i, who, b, near)
+
+    def sweep(blocks, nears, start, count, unroll):
+        mark(blocks, nears)
 
         def body(t, carry):
             attend(pl.multiple_of(t * (SUB * unroll), SUB * unroll), blocks, start, unroll)
@@ -272,13 +272,16 @@
     qcopy.wait_recv()
     sweep([(col, 2 * zh), (col, 2 * zh + 1)], [0.0] * 2, True, M, 4)
 
+    orders = by_lane(PLANES, y)
+    back_w, lane_w, gox_w, gop_w, gom_w = by_lane((BACK, LANE, GOX, GOP, GOM), y)
+
     def step_of(k):
-        back = pick(BACK, y, k)
-        who = (x - back) * 4 + pick(LANE, y, k)
+        back = pick(back_w, k)
+        who = (x - back) * 4 + pick(lane_w, k)
         there = x >= back
-        gox = there & (pick(GOX, y, k) > 0) & (x < 3)
-        gop = there & (pick(GOP, y, k) > 0)
-        gom = there & (pick(GOM, y, k) > 0)
+        gox = there & (pick(gox_w, k) > 0) & (x < 3)
+        gop = there & (pick(gop_w, k) > 0)
+        gom = there & (pick(gom_w, k) > 0)
         lone = there & (zh == 0) & (back == 2) & (who % 4 == y) & ((y < 3) | (x == 2))
         return who, there, gox, gop, gom, lone
 
@@ -291,39 +294,19 @@
             block_wait(rsem.at[who, b])
             hands(k + 1, who, b, gox, gop, gom)
 
-            @pl.when(lone & (b == 3) & (y < 3))
-            def _():
-                quarter(who, plus, 0).start()
-
             @pl.when(lone & (b == 3) & (y == 3))
             def _():
                 quarter(who, east, 0).start()
 
     corner = (zh == 0) & (x == 3)
 
-    def turn(i, carry):
-        op = fetch(y, i)
-
-        @pl.when(op < 32)
-        def _():
-            onward(op // 4, op % 4)
-
-        @pl.when((op >= 32) & (op < 64))
-        def _():
-            b = order(op % 4)
-            block_wait(zrecv.at[b])
-            hands(0, col, b, *own)
-
-        @pl.when((op == 64) & (zh == 1))
-        def _():
-            sweep([(col, 0), (col, 1)], [0.0] * 2, False, M, 4)
-
+    def pairs_of(op):
         blocks, nears, present = [], [], []
         for pair in ((op % 256) // 16, op % 16):
             who, there, gox, gop, gom, lone = step_of(pair // 2)
             pairs = [order(2 * (pair % 2) + j) for j in range(2)]
 
-            @pl.when((op >= 256) & there & jnp.logical_not(gox | gop | gom | lone))
+            @pl.when(there & jnp.logical_not(gox | gop | gom | lone))
             def _(who=who, pairs=pairs):
                 for b in pairs:
                     block_wait(rsem.at[who, b])
@@ -331,10 +314,36 @@
             blocks += [(jnp.where(there, who, col), b) for b in pairs]
             nears += [jnp.where(there, 0.0, -FAR)] * 2
             present.append(there)
-
-        @pl.when((op >= 256) & (present[0] | present[1]))
-        def _():
-            sweep(blocks, nears, False, M, 4)
+        return blocks, nears, present[0] | present[1]
+
+    def turn(i, carry):
+        op = fetch(orders, i)
+
+        @pl.when(op < 32)
+        def _():
+            onward(op // 4, op % 4)
+
+        @pl.when((op >= 32) & (op < 64))
+        def _():
+            b = order(op % 4)
+            block_wait(zrecv.at[b])
+            hands(0, col, b, *own)
+
+        @pl.when((op == 64) & (zh == 1))
+        def _():
+            sweep([(col, 0), (col, 1)], [0.0] * 2, False, M, 4)
+
+        @pl.when(op >= 256)
+        def _():
+            blocks, nears, present = pairs_of(op)
+
+            @pl.when(present)
+            def _():
+                sweep(blocks, nears, False, M, 4)
+
+        @pl.when((i == LATE) & (zh == 0) & (x >= 2) & (y < 3))
+        def _():
+            quarter(col - 8, plus, 0).start()
 
         @pl.when((i == RELAY) & corner & (y == 3))
         def _():
@@ -343,7 +352,8 @@
 
         return carry
 
-    lax.fori_loop(0, len(ORDER[0]), turn, 0)
+    last = len(ORDER[0]) - 1
+    lax.fori_loop(0, last, turn, 0)
 
     @pl.when(((zh == 0) & (x >= 2) & (y >= 1)) | (corner & (y == 0)))
     def _():
@@ -359,12 +369,31 @@
 
         lax.fori_loop(0, MC // 256, body, 0)
 
-    result(1 - c, obuf, 0)
     ocopy = pltpu.make_async_remote_copy(
         src_ref=obuf.at[0], dst_ref=o_ref.at[c],
         send_sem=osend, recv_sem=orecv, device_id=sibling, device_id_type=MESH)
-    ocopy.start()
-    result(c, o_ref, c)
+    blocks, nears, present = pairs_of(fetch(orders, last))
+    mark(blocks, nears)
+
+    def final(h, carry):
+        b = (1 - c + h) % 2
+
+        @pl.when(present)
+        def _():
+            attend(pl.multiple_of(b * MC, MC), blocks, False, MC // SUB)
+
+        @pl.when(h == 0)
+        def _():
+            result(b, obuf, 0)
+            ocopy.start()
+
+        @pl.when(h == 1)
+        def _():
+            result(b, o_ref, c)
+
+        return carry
+
+    lax.fori_loop(0, 2, final, 0)
     ocopy.wait_recv()
 
     ocopy.wait_send()
@@ -373,17 +402,22 @@
     pltpu.make_async_copy(kv.at[0, pl.ds(0, 2)], kv.at[0, pl.ds(0, 2)], zsend.at[1]).wait()
     handed(0, col, *own)
 
-    def drain(k, carry):
-        who, there, gox, gop, gom, lone = step_of(k)
-        handed(k + 1, who, gox, gop, gom)
-
-        @pl.when(lone)
-        def _():
-            block_wait(qtr.at[0])
-
-        return carry
-
-    lax.fori_loop(0, STEPS, drain, 0)
+    for lane in range(4):
+        @pl.when(y == lane)
+        def _(lane=lane):
+            for k, (back, _, gox, gop, gom) in enumerate(PLAN[lane]):
+                if gox or gop or gom:
+                    @pl.when(x >= back)
+                    def _(k=k, go=(gox, gop, gom)):
+                        for direction in range(3):
+                            if go[direction]:
+                                @pl.when((x < 3) | (direction > 0))
+                                def _(direction=direction):
+                                    pltpu.make_async_copy(kv.at[0], kv.at[0], ssem.at[k + 1, direction]).wait()
+
+    @pl.when((zh == 0) & ((x == 2) | ((x == 3) & (y < 3))))
+    def _():
+        block_wait(qtr.at[0])
 
     @pl.when(corner & (y == 3))
     def _():
@@ -401,7 +435,7 @@
         out_specs=vmem,
         scratch_shapes=[
             pltpu.VMEM((8 * PIECE, D), f32),
-            pltpu.VMEM((8, 2, PIECE, D), bf),
+            pltpu.VMEM((8, 2 * PIECE, D), bf),
             pltpu.VMEM((16, 4, CHUNK, D), bf),
             pltpu.VMEM((2, MC, 2 * D), bf),
             pltpu.VMEM((M, 2 * D), bf),

time: 67.8 us -> 64.7 us (0.954)
  the two profiles are of different devices: /device:TPU:39 before, /device:TPU:6 now
where the time goes in v4:
time: 64.7 us; the launch traced here: 64.6 us
  Pallas kernels  62.4 us (96%)
  local copies, waits for them, and re-layouts  2.15 us (3%)
    pallas_call x1, Pallas kernels, per_device(): pl.pallas_call(kernel, out_shape=jax.ShapeDtypeStruct((2, MC, D), bf), in...  62.4 us
    reshape x1, local copies, waits for them, and re-layouts, per_device(): jnp.swapaxes(out.reshape(2, ROWS, GROUP, D), 0, 1)  2.15 us

profile of v4, /device:TPU:6, one launch (start us, length us, event | category | flops | bytes accessed | tf_op | source)
XLA Modules:
  0.0 64.6 jit_solution(9931295881046783862)
XLA Ops:
  0.0 62.4 %shard_map.46 = bf16[2,1536,128]{2,1,0:T(8,128)(2,1)} custom-call(bf16[3072,128]{1,0:T(8,128)(2,1)} %bitcast.11, bf16[384,128]{1,0:T(8,128)(2,1)} %bitcast.12, bf16[384,128]{1,0:T(8,128)(2,1)} %bitcast.13, s32[1,192]{1,0:T(1,128)} %bitcast.14), custom_call_target="tpu_custom_call" | custom-call | tf_op jit(solution)/shard_map/pallas_call | solution.py:431
  62.4 2.1 %copy_bitcast_fusion = bf16[192,16,128]{2,1,0:T(8,128)(2,1)} fusion(bf16[2,1536,128]{2,1,0:T(8,128)(2,1)} %shard_map.46), kind=kLoop, calls=%fused_computation | loop fusion | bytes 1572864 | tf_op jit(solution)/shard_map/reshape | solution.py:454

commit v5 on v4

--- a/solution.py
+++ b/solution.py
@@ -24,24 +24,20 @@
 SCALE = (1.0 / math.sqrt(D)) * math.log2(math.e)
 
 PLAN = (
-    ((1, 0, 1, 1, 1), (1, 1, 0, 0, 1), (1, 3, 0, 1, 0), (2, 0, 0, 0, 0),
-     (1, 2, 0, 0, 0), (2, 1, 0, 0, 0), (2, 3, 0, 0, 0), (2, 2, 0, 0, 0)),
-    ((0, 0, 0, 1, 0), (1, 1, 1, 1, 1), (1, 0, 0, 0, 0), (1, 2, 0, 0, 0),
-     (2, 1, 0, 0, 1), (1, 3, 0, 0, 0), (2, 2, 0, 0, 1), (2, 3, 0, 0, 0)),
-    ((0, 1, 0, 1, 0), (1, 2, 1, 1, 1), (0, 0, 0, 0, 0), (1, 1, 0, 0, 0),
-     (1, 3, 0, 0, 0), (2, 2, 0, 0, 1), (1, 0, 0, 0, 0), (2, 3, 0, 0, 1)),
-    ((0, 2, 0, 0, 0), (0, 0, 0, 0, 0), (1, 3, 1, 1, 1), (0, 1, 0, 0, 0),
-     (1, 2, 0, 1, 0), (1, 0, 0, 0, 1), (2, 3, 0, 1, 1), (1, 1, 0, 0, 0)),
+    ((1, 0, 3, 1, 3), (1, 1, 2, 0, 1), (1, 3, 2, 3, 0), (2, 0, 0, 0, 0), (1, 2, 0, 0, 0), (2, 1, 0, 0, 0), (2, 3, 0, 0, 0), (2, 2, 0, 0, 0)),
+    ((0, 0, 2, 3, 0), (1, 1, 3, 1, 3), (1, 0, 0, 0, 0), (1, 2, 2, 0, 0), (2, 1, 0, 0, 1), (1, 3, 0, 0, 0), (2, 2, 0, 0, 3), (2, 3, 0, 0, 0)),
+    ((0, 1, 2, 3, 0), (1, 2, 3, 1, 3), (0, 0, 2, 0, 0), (1, 1, 0, 0, 0), (1, 3, 0, 0, 0), (2, 2, 0, 0, 1), (1, 0, 0, 0, 0), (2, 3, 0, 0, 3)),
+    ((0, 2, 2, 0, 0), (0, 0, 0, 0, 0), (1, 3, 3, 3, 3), (0, 1, 2, 0, 0), (1, 2, 0, 3, 0), (1, 0, 0, 0, 1), (2, 3, 0, 1, 3), (1, 1, 0, 0, 0)),
 )
 STEPS = len(PLAN[0])
-RELAY = 22
-LATE = 21
+RELAY = 23
+LATE = 22
 
 ORDER = (
-    (0, 1, 34, 35, 64, 4, 8, 5, 9, 258, 2, 12, 13, 326, 3, 282, 6, 10, 14, 15, 455, 7, 11, 309, 398, 445, 415),
-    (0, 4, 1, 5, 34, 258, 35, 64, 16, 17, 326, 2, 6, 24, 3, 7, 25, 385, 18, 316, 19, 377, 26, 421, 27, 475, 495),
-    (0, 4, 1, 5, 34, 258, 35, 64, 20, 21, 394, 6, 7, 28, 323, 2, 22, 364, 3, 23, 29, 283, 489, 30, 31, 343, 509),
-    (8, 9, 34, 258, 35, 64, 20, 24, 16, 21, 25, 330, 10, 454, 11, 17, 309, 26, 27, 385, 18, 22, 478, 19, 23, 411, 383),
+    (0, 1, 34, 8, 4, 35, 64, 9, 260, 5, 2, 12, 13, 354, 3, 282, 6, 14, 15, 455, 10, 7, 312, 11, 485, 445, 65, 505),
+    (0, 4, 1, 5, 34, 258, 16, 35, 64, 17, 326, 2, 6, 24, 7, 387, 25, 3, 18, 449, 15, 425, 27, 373, 26, 478, 65, 447),
+    (0, 4, 1, 5, 34, 258, 20, 35, 64, 21, 394, 6, 326, 7, 28, 2, 22, 316, 3, 29, 283, 487, 11, 30, 405, 31, 65, 509),
+    (8, 9, 34, 258, 20, 24, 35, 16, 64, 21, 25, 330, 10, 454, 17, 11, 26, 389, 3, 27, 305, 18, 22, 478, 19, 15, 441, 383),
 )
 
 
@@ -81,8 +77,8 @@
     return value
 
 
-def kernel(q_ref, k_ref, v_ref, id_ref, o_ref,
-           wide, snd, kv, qst, qaug, feat, ones, top, acc, obuf,
+def kernel(q_hbm, k_ref, v_ref, id_ref, o_ref,
+           q_ref, wide, snd, kv, qst, qaug, feat, ones, top, acc, obuf,
            zsend, zrecv, lsem, qsend, qrecv, osend, orecv, ssem, rsem, qtr):
     s = lax.axis_index("seq")
     g = lax.axis_index("head")
@@ -102,6 +98,9 @@
     minus = at(x, (y + 3) % 4)
     others = [(dz, dc, dg) for dz in (0, 1) for dc in (0, 1) for dg in (2, 1, 3, 0) if dz or dc or dg]
 
+    load = pltpu.make_async_copy(q_hbm, q_ref, lsem.at[2])
+    load.start()
+
     barrier = pltpu.get_barrier_semaphore()
     peers = [inside(*o) for o in others] + [east, at((x + 3) % 4, y), plus, minus]
     for peer in peers:
@@ -123,18 +122,23 @@
 
     spot = pl.ds(pl.multiple_of(2 * PIECE * g, 16), 2 * PIECE)
 
-    for o in others:
-        dz, dc, dg = o
-        head = 2 * ((g + dg) % 4) + (c + dc) % 2
-        pltpu.make_async_remote_copy(
-            src_ref=snd.at[head], dst_ref=kv.at[col, block, spot],
-            send_sem=zsend.at[dz], recv_sem=zrecv.at[block],
-            device_id=inside(*o), device_id_type=MESH).start()
-        if dg == 0:
+    def spread(plane):
+        for o in others:
+            dz, dc, dg = o
+            if dz != plane:
+                continue
+            head = 2 * ((g + dg) % 4) + (c + dc) % 2
             pltpu.make_async_remote_copy(
-                src_ref=kv.at[col, block, pl.ds(HALF, 16)], dst_ref=kv.at[col, block, pl.ds(HALF, 16)],
+                src_ref=snd.at[head], dst_ref=kv.at[col, block, spot],
                 send_sem=zsend.at[dz], recv_sem=zrecv.at[block],
                 device_id=inside(*o), device_id_type=MESH).start()
+            if dg == 0:
+                pltpu.make_async_remote_copy(
+                    src_ref=kv.at[col, block, pl.ds(HALF, 16)], dst_ref=kv.at[col, block, pl.ds(HALF, 16)],
+                    send_sem=zsend.at[dz], recv_sem=zrecv.at[block],
+                    device_id=inside(*o), device_id_type=MESH).start()
+
+    spread(0)
     pltpu.make_async_copy(snd.at[2 * g + c], kv.at[col, block, spot], lsem.at[0]).start()
 
     def wait_rows(sem, n):
@@ -155,6 +159,7 @@
                 rows[:, 8 * which:8 * which + 8, :].reshape(128, D).astype(jnp.bfloat16))
         return carry
 
+    load.wait()
     lax.fori_loop(0, ROWS // 16, split, 0)
     base = pl.multiple_of(c * MC, MC)
     qcopy = pltpu.make_async_remote_copy(
@@ -164,6 +169,8 @@
     qlocal = pltpu.make_async_copy(qst.at[c], qaug.at[pl.ds(base, MC)], lsem.at[1])
     qlocal.start()
     ones[...] = jnp.ones_like(ones)
+    wait_rows(zsend.at[0], 14 * PIECE + 16)
+    spread(1)
 
     def order(t):
         return 2 * ((zh + t // 2) % 2) + (c + t) % 2
@@ -275,26 +282,27 @@
     orders = by_lane(PLANES, y)
     back_w, lane_w, gox_w, gop_w, gom_w = by_lane((BACK, LANE, GOX, GOP, GOM), y)
 
-    def step_of(k):
+    def step_of(k, t):
+        bit = jnp.where(t == 3, 2, 1)
         back = pick(back_w, k)
         who = (x - back) * 4 + pick(lane_w, k)
         there = x >= back
-        gox = there & (pick(gox_w, k) > 0) & (x < 3)
-        gop = there & (pick(gop_w, k) > 0)
-        gom = there & (pick(gom_w, k) > 0)
-        lone = there & (zh == 0) & (back == 2) & (who % 4 == y) & ((y < 3) | (x == 2))
+        gox = there & ((pick(gox_w, k) & bit) > 0) & (x < 3)
+        gop = there & ((pick(gop_w, k) & bit) > 0)
+        gom = there & ((pick(gom_w, k) & bit) > 0)
+        lone = (zh == 0) & (x == 2) & (y == 3) & (who == 3)
         return who, there, gox, gop, gom, lone
 
     def onward(k, t):
-        who, there, gox, gop, gom, lone = step_of(k)
+        who, there, gox, gop, gom, lone = step_of(k, t)
         b = order(t)
 
-        @pl.when(gox | gop | gom | lone)
+        @pl.when(gox | gop | gom)
         def _():
             block_wait(rsem.at[who, b])
             hands(k + 1, who, b, gox, gop, gom)
 
-            @pl.when(lone & (b == 3) & (y == 3))
+            @pl.when(lone & (b == 3))
             def _():
                 quarter(who, east, 0).start()
 
@@ -303,12 +311,15 @@
     def pairs_of(op):
         blocks, nears, present = [], [], []
         for pair in ((op % 256) // 16, op % 16):
-            who, there, gox, gop, gom, lone = step_of(pair // 2)
-            pairs = [order(2 * (pair % 2) + j) for j in range(2)]
-
-            @pl.when(there & jnp.logical_not(gox | gop | gom | lone))
-            def _(who=who, pairs=pairs):
-                for b in pairs:
+            pairs = []
+            for j in range(2):
+                t = 2 * (pair % 2) + j
+                who, there, gox, gop, gom, lone = step_of(pair // 2, t)
+                b = order(t)
+                pairs.append(b)
+
+                @pl.when(there & jnp.logical_not(gox | gop | gom))
+                def _(who=who, b=b):
                     block_wait(rsem.at[who, b])
 
             blocks += [(jnp.where(there, who, col), b) for b in pairs]
@@ -398,7 +409,6 @@
 
     ocopy.wait_send()
     qcopy.wait_send()
-    wait_rows(zsend.at[0], 14 * PIECE + 16)
     pltpu.make_async_copy(kv.at[0, pl.ds(0, 2)], kv.at[0, pl.ds(0, 2)], zsend.at[1]).wait()
     handed(0, col, *own)
 
@@ -413,7 +423,8 @@
                             if go[direction]:
                                 @pl.when((x < 3) | (direction > 0))
                                 def _(direction=direction):
-                                    pltpu.make_async_copy(kv.at[0], kv.at[0], ssem.at[k + 1, direction]).wait()
+                                    some = kv.at[0, pl.ds(0, (0, 3, 1, 4)[go[direction]])]
+                                    pltpu.make_async_copy(some, some, ssem.at[k + 1, direction]).wait()
 
     @pl.when((zh == 0) & ((x == 2) | ((x == 3) & (y < 3))))
     def _():
@@ -431,9 +442,10 @@
     out = pl.pallas_call(
         kernel,
         out_shape=jax.ShapeDtypeStruct((2, MC, D), bf),
-        in_specs=[vmem] * 4,
+        in_specs=[pl.BlockSpec(memory_space=pl.ANY)] + [vmem] * 3,
         out_specs=vmem,
         scratch_shapes=[
+            pltpu.VMEM((ROWS * 16, D), bf),
             pltpu.VMEM((8 * PIECE, D), f32),
             pltpu.VMEM((8, 2 * PIECE, D), bf),
             pltpu.VMEM((16, 4, CHUNK, D), bf),
@@ -444,7 +456,7 @@
             pltpu.VMEM((M, D), f32),
             pltpu.VMEM((M, 2 * D), f32),
             pltpu.VMEM((1, MC, D), bf),
-            dma((2,)), dma((4,)), dma((2,)), dma, dma, dma, dma,
+            dma((2,)), dma((4,)), dma((3,)), dma, dma, dma, dma,
             dma((STEPS + 1, 3)), dma((16, 4)), dma((2,)),
         ],
         compiler_params=pltpu.CompilerParams(

time: 64.7 us -> 62.8 us (0.971)
  the two profiles are of different devices: /device:TPU:6 before, /device:TPU:39 now
where the time goes in v5:
time: 62.8 us; the launch traced here: 62.7 us
  Pallas kernels  60.5 us (96%)
  local copies, waits for them, and re-layouts  2.15 us (3%)
    pallas_call x1, Pallas kernels, per_device(): pl.pallas_call(kernel, out_shape=jax.ShapeDtypeStruct((2, MC, D), bf), in...  60.5 us
    reshape x1, local copies, waits for them, and re-layouts, per_device(): jnp.swapaxes(out.reshape(2, ROWS, GROUP, D), 0, 1)  2.15 us

profile of v5, /device:TPU:39, one launch (start us, length us, event | category | flops | bytes accessed | tf_op | source)
XLA Modules:
  0.0 62.7 jit_solution(16106383752831056029)
XLA Ops:
  0.0 60.5 %shard_map.46 = bf16[2,1536,128]{2,1,0:T(8,128)(2,1)} custom-call(bf16[3072,128]{1,0:T(8,128)(2,1)} %bitcast.11, bf16[384,128]{1,0:T(8,128)(2,1)} %bitcast.12, bf16[384,128]{1,0:T(8,128)(2,1)} %bitcast.13, s32[1,192]{1,0:T(1,128)} %bitcast.14), custom_call_target="tpu_custom_call" | custom-call | tf_op jit(solution)/shard_map/pallas_call | solution.py:442
  60.5 2.1 %copy_bitcast_fusion = bf16[192,16,128]{2,1,0:T(8,128)(2,1)} fusion(bf16[2,1536,128]{2,1,0:T(8,128)(2,1)} %shard_map.46), kind=kLoop, calls=%fused_computation | loop fusion | bytes 1572864 | tf_op jit(solution)/shard_map/reshape | solution.py:466

commit v6 on v5

--- a/solution.py
+++ b/solution.py
@@ -117,6 +117,29 @@
     tile = jnp.concatenate([first, second, jnp.zeros((14, D), jnp.float32)], axis=0)
     block = 2 * zh + c
     kv[col, block, HALF:, :] = tile.astype(jnp.bfloat16)
+
+    turned = jnp.transpose(tile[:8])
+    lanes = lax.broadcasted_iota(jnp.int32, (D, D), 1).astype(jnp.float32)
+    def queries():
+        for part, size in ((0, D), (1, ROWS - D)):
+            hot = jnp.where(turned[:size, part:part + 1] == lanes[:size], 1.0, 0.0)
+            hot = jnp.broadcast_to(hot[:, None, :], (size, GROUP, D)).reshape(size * GROUP, D)
+            for which in range(2):
+                qst[which, pl.ds(part * D * GROUP, size * GROUP), D:] = hot.astype(jnp.bfloat16)
+
+        def split(t, carry):
+            rows = q_ref[pl.ds(t * 16 * 16, 256), :].astype(jnp.float32).reshape(16, 16, D)
+            for which in range(2):
+                qst[which, pl.ds(t * 128, 128), :D] = (
+                    rows[:, 8 * which:8 * which + 8, :].reshape(128, D).astype(jnp.bfloat16))
+            return carry
+
+        load.wait()
+        lax.fori_loop(0, ROWS // 16, split, 0)
+
+    @pl.when(zh == 0)
+    def _():
+        queries()
 
     pl.semaphore_wait(barrier, len(peers))
 
@@ -139,28 +162,16 @@
                     device_id=inside(*o), device_id_type=MESH).start()
 
     spread(0)
+    spread(1)
     pltpu.make_async_copy(snd.at[2 * g + c], kv.at[col, block, spot], lsem.at[0]).start()
 
     def wait_rows(sem, n):
         pltpu.make_async_copy(feat.at[pl.ds(0, n)], feat.at[pl.ds(0, n)], sem).wait()
 
-    turned = jnp.transpose(tile[:8])
-    lanes = lax.broadcasted_iota(jnp.int32, (D, D), 1).astype(jnp.float32)
-    for part, size in ((0, D), (1, ROWS - D)):
-        hot = jnp.where(turned[:size, part:part + 1] == lanes[:size], 1.0, 0.0)
-        hot = jnp.broadcast_to(hot[:, None, :], (size, GROUP, D)).reshape(size * GROUP, D)
-        for which in range(2):
-            qst[which, pl.ds(part * D * GROUP, size * GROUP), D:] = hot.astype(jnp.bfloat16)
-
-    def split(t, carry):
-        rows = q_ref[pl.ds(t * 16 * 16, 256), :].astype(jnp.float32).reshape(16, 16, D)
-        for which in range(2):
-            qst[which, pl.ds(t * 128, 128), :D] = (
-                rows[:, 8 * which:8 * which + 8, :].reshape(128, D).astype(jnp.bfloat16))
-        return carry
-
-    load.wait()
-    lax.fori_loop(0, ROWS // 16, split, 0)
+    @pl.when(zh == 1)
+    def _():
+        queries()
+
     base = pl.multiple_of(c * MC, MC)
     qcopy = pltpu.make_async_remote_copy(
         src_ref=qst.at[1 - c], dst_ref=qaug.at[pl.ds(base, MC)],
@@ -169,8 +180,6 @@
     qlocal = pltpu.make_async_copy(qst.at[c], qaug.at[pl.ds(base, MC)], lsem.at[1])
     qlocal.start()
     ones[...] = jnp.ones_like(ones)
-    wait_rows(zsend.at[0], 14 * PIECE + 16)
-    spread(1)
 
     def order(t):
         return 2 * ((zh + t // 2) % 2) + (c + t) % 2
@@ -409,6 +418,7 @@
 
     ocopy.wait_send()
     qcopy.wait_send()
+    wait_rows(zsend.at[0], 14 * PIECE + 16)
     pltpu.make_async_copy(kv.at[0, pl.ds(0, 2)], kv.at[0, pl.ds(0, 2)], zsend.at[1]).wait()
     handed(0, col, *own)
 

time: 62.8 us -> 64.7 us (1.030)
  the two profiles are of different devices: /device:TPU:39 before, /device:TPU:6 now
where the time goes in v6:
time: 64.7 us; the launch traced here: 64.5 us
  Pallas kernels  62.3 us (96%)
  local copies, waits for them, and re-layouts  2.15 us (3%)
    pallas_call x1, Pallas kernels, per_device(): pl.pallas_call(kernel, out_shape=jax.ShapeDtypeStruct((2, MC, D), bf), in...  62.3 us
    reshape x1, local copies, waits for them, and re-layouts, per_device(): jnp.swapaxes(out.reshape(2, ROWS, GROUP, D), 0, 1)  2.15 us

profile of v6, /device:TPU:6, one launch (start us, length us, event | category | flops | bytes accessed | tf_op | source)
XLA Modules:
  0.0 64.5 jit_solution(9500462699536248732)
XLA Ops:
  0.0 62.3 %shard_map.46 = bf16[2,1536,128]{2,1,0:T(8,128)(2,1)} custom-call(bf16[3072,128]{1,0:T(8,128)(2,1)} %bitcast.11, bf16[384,128]{1,0:T(8,128)(2,1)} %bitcast.12, bf16[384,128]{1,0:T(8,128)(2,1)} %bitcast.13, s32[1,192]{1,0:T(1,128)} %bitcast.14), custom_call_target="tpu_custom_call" | custom-call | tf_op jit(solution)/shard_map/pallas_call | solution.py:452
  62.4 2.1 %copy_bitcast_fusion = bf16[192,16,128]{2,1,0:T(8,128)(2,1)} fusion(bf16[2,1536,128]{2,1,0:T(8,128)(2,1)} %shard_map.46), kind=kLoop, calls=%fused_computation | loop fusion | bytes 1572864 | tf_op jit(solution)/shard_map/reshape | solution.py:476

commit v7 on v6

--- a/solution.py
+++ b/solution.py
@@ -161,8 +161,14 @@
                     send_sem=zsend.at[dz], recv_sem=zrecv.at[block],
                     device_id=inside(*o), device_id_type=MESH).start()
 
-    spread(0)
-    spread(1)
+    @pl.when(zh == 0)
+    def _():
+        spread(0)
+
+    @pl.when(zh == 1)
+    def _():
+        spread(1)
+
     pltpu.make_async_copy(snd.at[2 * g + c], kv.at[col, block, spot], lsem.at[0]).start()
 
     def wait_rows(sem, n):
@@ -171,6 +177,7 @@
     @pl.when(zh == 1)
     def _():
         queries()
+        spread(0)
 
     base = pl.multiple_of(c * MC, MC)
     qcopy = pltpu.make_async_remote_copy(
@@ -180,6 +187,12 @@
     qlocal = pltpu.make_async_copy(qst.at[c], qaug.at[pl.ds(base, MC)], lsem.at[1])
     qlocal.start()
     ones[...] = jnp.ones_like(ones)
+
+    @pl.when(zh == 0)
+    def _():
+        wait_rows(zsend.at[0], 14 * PIECE + 16)
+        spread(1)
+
 
     def order(t):
         return 2 * ((zh + t // 2) % 2) + (c + t) % 2
@@ -418,7 +431,10 @@
 
     ocopy.wait_send()
     qcopy.wait_send()
-    wait_rows(zsend.at[0], 14 * PIECE + 16)
+    @pl.when(zh == 1)
+    def _():
+        wait_rows(zsend.at[0], 14 * PIECE + 16)
+
     pltpu.make_async_copy(kv.at[0, pl.ds(0, 2)], kv.at[0, pl.ds(0, 2)], zsend.at[1]).wait()
     handed(0, col, *own)
 

time: 64.7 us -> 62.3 us (0.963)
  the two profiles are of different devices: /device:TPU:6 before, /device:TPU:39 now
where the time goes in v7:
time: 62.3 us; the launch traced here: 61.4 us
  Pallas kernels  59.2 us (95%)
  local copies, waits for them, and re-layouts  2.15 us (3%)
    pallas_call x1, Pallas kernels, per_device(): pl.pallas_call(kernel, out_shape=jax.ShapeDtypeStruct((2, MC, D), bf), in...  59.2 us
    reshape x1, local copies, waits for them, and re-layouts, per_device(): jnp.swapaxes(out.reshape(2, ROWS, GROUP, D), 0, 1)  2.15 us

profile of v7, /device:TPU:39, one launch (start us, length us, event | category | flops | bytes accessed | tf_op | source)
XLA Modules:
  0.0 61.4 jit_solution(17051707752620482580)
XLA Ops:
  0.0 59.2 %shard_map.46 = bf16[2,1536,128]{2,1,0:T(8,128)(2,1)} custom-call(bf16[3072,128]{1,0:T(8,128)(2,1)} %bitcast.11, bf16[384,128]{1,0:T(8,128)(2,1)} %bitcast.12, bf16[384,128]{1,0:T(8,128)(2,1)} %bitcast.13, s32[1,192]{1,0:T(1,128)} %bitcast.14), custom_call_target="tpu_custom_call" | custom-call | tf_op jit(solution)/shard_map/pallas_call | solution.py:468
  59.2 2.1 %copy_bitcast_fusion = bf16[192,16,128]{2,1,0:T(8,128)(2,1)} fusion(bf16[2,1536,128]{2,1,0:T(8,128)(2,1)} %shard_map.46), kind=kLoop, calls=%fused_computation | loop fusion | bytes 1572864 | tf_op jit(solution)/shard_map/reshape | solution.py:492
